TPU v7x, 32 devices: a whole 2x2x4 slice. The times are simulated.
32 devices in a mesh: rep: 8 (over y, x, core), shard: 4 (over z).
Axes of the slice: x: 2, y: 2, z: 4, core: 2. Of those that a mesh axis runs over, the one named last changes fastest.
Arguments:
- tokens: bfloat16 [6144, 768], P(('rep', 'shard')), may hold values from -6 to 6
- seq_len: int32 [8, 8], P('rep'), may hold values from 1 to 672, as said below
- norm_gain: bfloat16 [2, 2, 768], P(None, None, 'shard'), may hold values from 0.5 to 1.5
- norm_bias: bfloat16 [2, 2, 768], P(None, None, 'shard'), may hold values from -1.5 to 1.5
- w_qkv: bfloat16 [2, 768, 2304], P(None, 'shard'), may hold values from -0.21875 to 0.21875
- b_qkv: bfloat16 [2, 2304], P(None, 'shard'), may hold values from -1.5 to 1.5
- w_out: bfloat16 [2, 768, 768], P(None, 'shard'), may hold values from -1.75 to 1.75
- b_out: bfloat16 [2, 768], P(None, 'shard'), may hold values from -1.5 to 1.5
- w_up: bfloat16 [2, 768, 3072], P(None, 'shard'), may hold values from -0.21875 to 0.21875
- b_up: bfloat16 [2, 3072], P(None, 'shard'), may hold values from -1.5 to 1.5
- w_down: bfloat16 [2, 3072, 768], P(None, 'shard'), may hold values from -0.109375 to 0.109375
- b_down: bfloat16 [2, 768], P(None, 'shard'), may hold values from -1.5 to 1.5
- cotangent: float32 [6144, 768], P(('rep', 'shard')), may hold values from -6 to 6
Outputs:
- output: float32 [6144, 768], P(('rep', 'shard'))
- grad_tokens: float32 [6144, 768], P(('rep', 'shard'))
- grad_norm_gain: float32 [2, 2, 768], P(None, None, 'shard')
- grad_norm_bias: float32 [2, 2, 768], P(None, None, 'shard')
- grad_w_qkv: float32 [2, 768, 2304], P(None, 'shard')
- grad_b_qkv: float32 [2, 2304], P(None, 'shard')
- grad_w_out: float32 [2, 768, 768], P(None, 'shard')
- grad_b_out: float32 [2, 768], P(None, 'shard')
- grad_w_up: float32 [2, 768, 3072], P(None, 'shard')
- grad_b_up: float32 [2, 3072], P(None, 'shard')
- grad_w_down: float32 [2, 3072, 768], P(None, 'shard')
- grad_b_down: float32 [2, 768], P(None, 'shard')
Inputs may be any that keep to these rules, and one draw needn't show every extreme that they name: `seq_len`: row r holds the lengths of replica group r's 8 sequences in order; they sum to 768; the second is exactly 672 long and the first is at most 48 long.
All inputs are finite; a program needn't handle non-finite values.
Results may differ from a plain program's by a relative error of at most 0.015.
Values may be sent and summed in bfloat16 or wider, within the bound.
A program may use at most 192 MiB of HBM per device.

v0:
```python
import math

import jax
import jax.numpy as jnp
from jax import lax
from jax.sharding import PartitionSpec as P

HEADS = 12
HEAD = 64
ROT = 16
LAYERS = 2


EPSILON = 1e-05
MASKED = -1e30


def layer_norm(values, gain, shift):
    center = values - jnp.mean(values, axis=-1, keepdims=True)
    spread = jnp.mean(center * center, axis=-1, keepdims=True)
    return center * lax.rsqrt(spread + EPSILON) * gain + shift


def sequence_layout(lengths, total):
    ends = jnp.cumsum(lengths, dtype=jnp.int32)
    starts = ends - lengths
    offsets = jnp.arange(total, dtype=jnp.int32)
    after = offsets[:, None] >= starts[None, :]
    doc_ids = jnp.sum(after.astype(jnp.int32), axis=1, dtype=jnp.int32) - 1
    begins = jnp.max(jnp.where(after, starts[None, :], 0), axis=1)
    return (doc_ids, offsets - begins)


def rotary_tables(places):
    inverse = jnp.exp(jnp.arange(ROT // 2, dtype=jnp.float32) * (-2.0 * math.log(10000.0) / ROT))
    angles = places.astype(jnp.float32)[:, None] * inverse[None, :]
    return (jnp.cos(angles), jnp.sin(angles))


def rotate(field, cosine, sine):
    half = ROT // 2
    leading = field[..., :half]
    trailing = field[..., half:ROT]
    cos_rows = cosine[:, None, :]
    sin_rows = sine[:, None, :]
    return jnp.concatenate(
        [
            leading * cos_rows - trailing * sin_rows,
            trailing * cos_rows + leading * sin_rows,
            field[..., ROT:],
        ],
        axis=-1,
    )


def score_block(queries, key_block, query_doc, query_pos, key_doc, key_pos, score_scale):
    scores = (
        jnp.einsum("qhd,khd->hqk", queries, key_block, preferred_element_type=jnp.float32)
        * score_scale
    )
    allowed = (query_doc[:, None] == key_doc[None, :]) & (query_pos[:, None] >= key_pos[None, :])
    return jnp.where(allowed[None], scores, MASKED)


def attend_forward(
    queries, key_blocks, value_blocks, query_doc, query_pos, doc_blocks, pos_blocks, score_scale
):
    local_rows = queries.shape[0]
    blocks_in = (key_blocks, value_blocks, doc_blocks, pos_blocks)

    def collect_stats(carry, items):
        running_max, running_sum = carry
        key_block, value_block, key_doc, key_pos = items
        scores = score_block(
            queries, key_block, query_doc, query_pos, key_doc, key_pos, score_scale
        )
        new_max = jnp.maximum(running_max, jnp.max(scores, axis=-1))
        running_sum = running_sum * jnp.exp(running_max - new_max) + jnp.sum(
            jnp.exp(scores - new_max[..., None]), axis=-1
        )
        return ((new_max, running_sum), None)

    start_stats = (
        jnp.full((HEADS, local_rows), MASKED, jnp.float32),
        jnp.zeros((HEADS, local_rows), jnp.float32),
    )
    (top_score, total_sum), _ = lax.scan(collect_stats, start_stats, blocks_in)
    log_total = top_score + jnp.log(total_sum)

    def apply_weights(carry, items):
        rounded_sum, remainder_sum = carry
        key_block, value_block, key_doc, key_pos = items
        scores = score_block(
            queries, key_block, query_doc, query_pos, key_doc, key_pos, score_scale
        )
        weights = jnp.exp(scores - log_total[..., None])
        upper = weights.astype(jnp.bfloat16)
        lower = (weights - upper.astype(jnp.float32)).astype(jnp.bfloat16)
        rounded_sum = rounded_sum + jnp.einsum(
            "hqk,khd->qhd", upper, value_block, preferred_element_type=jnp.float32
        )
        remainder_sum = remainder_sum + jnp.einsum(
            "hqk,khd->qhd", lower, value_block, preferred_element_type=jnp.float32
        )
        return ((rounded_sum, remainder_sum), None)

    zero_out = jnp.zeros(queries.shape, jnp.float32)
    (attended, remainder), _ = lax.scan(apply_weights, (zero_out, zero_out), blocks_in)
    return (attended, log_total, attended + remainder)


def attend_backward(
    queries,
    key_blocks,
    value_blocks,
    grad_out,
    log_total,
    delta,
    query_doc,
    query_pos,
    doc_blocks,
    pos_blocks,
    score_scale,
):

    def step_back(grad_query, items):
        key_block, value_block, key_doc, key_pos = items
        scores = score_block(
            queries, key_block, query_doc, query_pos, key_doc, key_pos, score_scale
        )
        weights = jnp.exp(scores - log_total[..., None])
        grad_weights = jnp.einsum(
            "qhd,khd->hqk", grad_out, value_block, preferred_element_type=jnp.float32
        )
        grad_scores = (weights * (grad_weights - delta[..., None])).astype(jnp.bfloat16)
        grad_query = (
            grad_query
            + jnp.einsum("hqk,khd->qhd", grad_scores, key_block, preferred_element_type=jnp.float32)
            * score_scale
        )
        grad_value = jnp.einsum(
            "hqk,qhd->khd",
            weights.astype(jnp.bfloat16),
            grad_out,
            preferred_element_type=jnp.float32,
        )
        grad_key = (
            jnp.einsum("hqk,qhd->khd", grad_scores, queries, preferred_element_type=jnp.float32)
            * score_scale
        )
        return (grad_query, (grad_key, grad_value))

    grad_query, outputs = lax.scan(
        step_back,
        jnp.zeros(queries.shape, jnp.float32),
        (key_blocks, value_blocks, doc_blocks, pos_blocks),
    )
    return (grad_query, outputs[0].reshape(-1, HEADS * HEAD), outputs[1].reshape(-1, HEADS * HEAD))


def per_device(
    tokens,
    seq_len,
    norm_gain,
    norm_bias,
    w_qkv,
    b_qkv,
    w_out,
    b_out,
    w_up,
    b_up,
    w_down,
    b_down,
    cotangent,
):
    shards = lax.axis_size("shard")
    device_rank = lax.axis_index("shard")
    local_rows = tokens.shape[0]
    model_width = w_out.shape[2]
    group_rows = local_rows * shards
    doc_ids, places = sequence_layout(seq_len[0], group_rows)
    group_pos = jnp.arange(group_rows, dtype=jnp.int32)
    first_row = device_rank * local_rows
    query_doc = lax.dynamic_slice_in_dim(doc_ids, first_row, local_rows)
    query_pos = lax.dynamic_slice_in_dim(group_pos, first_row, local_rows)
    query_place = lax.dynamic_slice_in_dim(places, first_row, local_rows)
    cosine, sine = rotary_tables(query_place)
    factor = 1
    while factor * local_rows < 512 and shards % (factor * 2) == 0:
        factor = factor * 2
    block_rows = factor * local_rows
    block_count = group_rows // block_rows
    doc_blocks = doc_ids.reshape(block_count, block_rows)
    pos_blocks = group_pos.reshape(block_count, block_rows)
    score_scale = 1.0 / math.sqrt(HEAD)

    def as_blocks(array):
        return array.reshape(block_count, block_rows, HEADS, HEAD)

    resid = tokens.astype(jnp.float32)
    stored = []
    for layer_index in range(LAYERS):
        params = (
            lax.all_gather(norm_gain[layer_index], "shard", axis=1, tiled=True),
            lax.all_gather(norm_bias[layer_index], "shard", axis=1, tiled=True),
            lax.all_gather(w_qkv[layer_index], "shard", axis=0, tiled=True),
            lax.all_gather(b_qkv[layer_index], "shard", axis=0, tiled=True),
            lax.all_gather(w_out[layer_index], "shard", axis=0, tiled=True),
            lax.all_gather(b_out[layer_index], "shard", axis=0, tiled=True),
            lax.all_gather(w_up[layer_index], "shard", axis=0, tiled=True),
            lax.all_gather(b_up[layer_index], "shard", axis=0, tiled=True),
            lax.all_gather(w_down[layer_index], "shard", axis=0, tiled=True),
            lax.all_gather(b_down[layer_index], "shard", axis=0, tiled=True),
        )
        (
            gains,
            shifts,
            weight_qkv,
            bias_qkv,
            weight_out,
            bias_out,
            weight_up,
            bias_up,
            weight_down,
            bias_down,
        ) = params
        normed_one = layer_norm(
            resid, gains[0].astype(jnp.float32), shifts[0].astype(jnp.float32)
        ).astype(jnp.bfloat16)
        normed_two = layer_norm(
            resid, gains[1].astype(jnp.float32), shifts[1].astype(jnp.float32)
        ).astype(jnp.bfloat16)
        mixed = jnp.dot(
            normed_one, weight_qkv, preferred_element_type=jnp.float32
        ) + bias_qkv.astype(jnp.float32)
        queries = rotate(
            mixed[:, :model_width].reshape(local_rows, HEADS, HEAD), cosine, sine
        ).astype(jnp.bfloat16)
        key_rows = (
            rotate(
                mixed[:, model_width : 2 * model_width].reshape(local_rows, HEADS, HEAD),
                cosine,
                sine,
            )
            .astype(jnp.bfloat16)
            .reshape(local_rows, model_width)
        )
        value_rows = mixed[:, 2 * model_width :].astype(jnp.bfloat16)
        key_all, value_all = (
            lax.all_gather(key_rows, "shard", axis=0, tiled=True),
            lax.all_gather(value_rows, "shard", axis=0, tiled=True),
        )
        attended, log_total, exact_out = attend_forward(
            queries,
            as_blocks(key_all),
            as_blocks(value_all),
            query_doc,
            query_pos,
            doc_blocks,
            pos_blocks,
            score_scale,
        )
        attended16 = attended.reshape(local_rows, model_width).astype(jnp.bfloat16)
        branch_attn = jnp.dot(
            attended16, weight_out, preferred_element_type=jnp.float32
        ) + bias_out.astype(jnp.float32)
        hidden = jnp.dot(
            normed_two, weight_up, preferred_element_type=jnp.float32
        ) + bias_up.astype(jnp.float32)
        active16 = jax.nn.gelu(hidden, approximate=False).astype(jnp.bfloat16)
        branch_mlp = jnp.dot(
            active16, weight_down, preferred_element_type=jnp.float32
        ) + bias_down.astype(jnp.float32)
        stored.append(
            (
                resid,
                normed_one,
                normed_two,
                queries,
                key_rows,
                value_rows,
                key_all,
                value_all,
                attended16,
                log_total,
                exact_out,
                hidden,
                active16,
                params,
            )
        )
        resid = resid + branch_attn + branch_mlp
    gradient = cotangent
    layer_grads = []
    for layer_index in range(LAYERS - 1, -1, -1):
        (
            resid_in,
            normed_one,
            normed_two,
            queries,
            key_rows,
            value_rows,
            key_all,
            value_all,
            attended16,
            log_total,
            exact_out,
            hidden,
            active16,
            params,
        ) = stored[layer_index]
        weights = (
            lax.all_gather(norm_gain[layer_index], "shard", axis=1, tiled=True),
            lax.all_gather(norm_bias[layer_index], "shard", axis=1, tiled=True),
            lax.all_gather(w_qkv[layer_index], "shard", axis=0, tiled=True),
            lax.all_gather(b_qkv[layer_index], "shard", axis=0, tiled=True),
            lax.all_gather(w_out[layer_index], "shard", axis=0, tiled=True),
            lax.all_gather(b_out[layer_index], "shard", axis=0, tiled=True),
            lax.all_gather(w_up[layer_index], "shard", axis=0, tiled=True),
            lax.all_gather(b_up[layer_index], "shard", axis=0, tiled=True),
            lax.all_gather(w_down[layer_index], "shard", axis=0, tiled=True),
            lax.all_gather(b_down[layer_index], "shard", axis=0, tiled=True),
        )
        key_again, value_again = (
            lax.all_gather(key_rows, "shard", axis=0, tiled=True),
            lax.all_gather(value_rows, "shard", axis=0, tiled=True),
        )
        (
            gains,
            shifts,
            weight_qkv,
            bias_qkv,
            weight_out,
            bias_out,
            weight_up,
            bias_up,
            weight_down,
            bias_down,
        ) = weights
        grad16 = gradient.astype(jnp.bfloat16)
        grad_bias_sum = jnp.sum(grad16, axis=0, dtype=jnp.float32)
        grad_w_attn = jnp.dot(attended16.T, grad16, preferred_element_type=jnp.float32)
        grad_w_back = jnp.dot(active16.T, grad16, preferred_element_type=jnp.float32)
        grad_attended = (
            jnp.dot(grad16, weight_out.T, preferred_element_type=jnp.float32)
            .astype(jnp.bfloat16)
            .reshape(local_rows, HEADS, HEAD)
        )
        grad_active = jnp.dot(grad16, weight_down.T, preferred_element_type=jnp.float32)
        _, gelu_pull = jax.vjp(lambda values: jax.nn.gelu(values, approximate=False), hidden)
        grad_hidden = gelu_pull(grad_active)[0].astype(jnp.bfloat16)
        grad_w_hidden = jnp.dot(normed_two.T, grad_hidden, preferred_element_type=jnp.float32)
        grad_b_hidden = jnp.sum(grad_hidden, axis=0, dtype=jnp.float32)
        grad_second = jnp.dot(grad_hidden, weight_up.T, preferred_element_type=jnp.float32)
        delta = jnp.sum(grad_attended.astype(jnp.float32) * exact_out, axis=-1).T
        grad_query, grad_keys_all, grad_values_all = attend_backward(
            queries,
            as_blocks(key_again),
            as_blocks(value_again),
            grad_attended,
            log_total,
            delta,
            query_doc,
            query_pos,
            doc_blocks,
            pos_blocks,
            score_scale,
        )
        grad_keys, grad_values = (
            lax.psum_scatter(
                grad_keys_all.astype(jnp.bfloat16), "shard", scatter_dimension=0, tiled=True
            ).astype(jnp.float32),
            lax.psum_scatter(
                grad_values_all.astype(jnp.bfloat16), "shard", scatter_dimension=0, tiled=True
            ).astype(jnp.float32),
        )
        grad_query_pre = rotate(grad_query, cosine, -sine).reshape(local_rows, model_width)
        grad_keys_pre = rotate(grad_keys.reshape(local_rows, HEADS, HEAD), cosine, -sine).reshape(
            local_rows, model_width
        )
        grad_mixed = jnp.concatenate([grad_query_pre, grad_keys_pre, grad_values], axis=1).astype(
            jnp.bfloat16
        )
        grad_w_mixed = jnp.dot(normed_one.T, grad_mixed, preferred_element_type=jnp.float32)
        grad_b_mixed = jnp.sum(grad_mixed, axis=0, dtype=jnp.float32)
        grad_first = jnp.dot(grad_mixed, weight_qkv.T, preferred_element_type=jnp.float32)
        _, pull_one = jax.vjp(
            layer_norm, resid_in, gains[0].astype(jnp.float32), shifts[0].astype(jnp.float32)
        )
        _, pull_two = jax.vjp(
            layer_norm, resid_in, gains[1].astype(jnp.float32), shifts[1].astype(jnp.float32)
        )
        back_one = pull_one(grad_first)
        back_two = pull_two(grad_second)
        grad_gains = jnp.stack([back_one[1], back_two[1]])
        grad_shifts = jnp.stack([back_one[2], back_two[2]])
        gradient = gradient + back_one[0] + back_two[0]
        reduced = (
            lax.psum_scatter(
                grad_gains.astype(jnp.bfloat16), "shard", scatter_dimension=1, tiled=True
            ).astype(jnp.float32),
            lax.psum_scatter(
                grad_shifts.astype(jnp.bfloat16), "shard", scatter_dimension=1, tiled=True
            ).astype(jnp.float32),
            lax.psum_scatter(
                grad_w_mixed.astype(jnp.bfloat16), "shard", scatter_dimension=0, tiled=True
            ).astype(jnp.float32),
            lax.psum_scatter(
                grad_b_mixed.astype(jnp.bfloat16), "shard", scatter_dimension=0, tiled=True
            ).astype(jnp.float32),
            lax.psum_scatter(
                grad_w_attn.astype(jnp.bfloat16), "shard", scatter_dimension=0, tiled=True
            ).astype(jnp.float32),
            lax.psum_scatter(
                grad_bias_sum.astype(jnp.bfloat16), "shard", scatter_dimension=0, tiled=True
            ).astype(jnp.float32),
            lax.psum_scatter(
                grad_w_hidden.astype(jnp.bfloat16), "shard", scatter_dimension=0, tiled=True
            ).astype(jnp.float32),
            lax.psum_scatter(
                grad_b_hidden.astype(jnp.bfloat16), "shard", scatter_dimension=0, tiled=True
            ).astype(jnp.float32),
            lax.psum_scatter(
                grad_w_back.astype(jnp.bfloat16), "shard", scatter_dimension=0, tiled=True
            ).astype(jnp.float32),
            lax.psum_scatter(
                grad_bias_sum.astype(jnp.bfloat16), "shard", scatter_dimension=0, tiled=True
            ).astype(jnp.float32),
        )
        reduced = (
            lax.psum(reduced[0].astype(jnp.bfloat16), "rep").astype(jnp.float32),
            lax.psum(reduced[1].astype(jnp.bfloat16), "rep").astype(jnp.float32),
            lax.psum(reduced[2].astype(jnp.bfloat16), "rep").astype(jnp.float32),
            lax.psum(reduced[3].astype(jnp.bfloat16), "rep").astype(jnp.float32),
            lax.psum(reduced[4].astype(jnp.bfloat16), "rep").astype(jnp.float32),
            lax.psum(reduced[5].astype(jnp.bfloat16), "rep").astype(jnp.float32),
            lax.psum(reduced[6].astype(jnp.bfloat16), "rep").astype(jnp.float32),
            lax.psum(reduced[7].astype(jnp.bfloat16), "rep").astype(jnp.float32),
            lax.psum(reduced[8].astype(jnp.bfloat16), "rep").astype(jnp.float32),
            lax.psum(reduced[9].astype(jnp.bfloat16), "rep").astype(jnp.float32),
        )
        layer_grads.append(reduced)
    layer_grads = layer_grads[::-1]
    stacked = [
        jnp.stack([layer_grads[layer_pos][member] for layer_pos in range(LAYERS)])
        for member in range(10)
    ]
    return (
        resid,
        gradient,
        stacked[0],
        stacked[1],
        stacked[2],
        stacked[3],
        stacked[4],
        stacked[5],
        stacked[6],
        stacked[7],
        stacked[8],
        stacked[9],
    )


def solution(mesh):
    return jax.shard_map(
        per_device,
        mesh=mesh,
        in_specs=(
            P(("rep", "shard"), None),
            P("rep", None),
            P(None, None, "shard"),
            P(None, None, "shard"),
            P(None, "shard", None),
            P(None, "shard"),
            P(None, "shard", None),
            P(None, "shard"),
            P(None, "shard", None),
            P(None, "shard"),
            P(None, "shard", None),
            P(None, "shard"),
            P(("rep", "shard"), None),
        ),
        out_specs=(
            P(("rep", "shard"), None),
            P(("rep", "shard"), None),
            P(None, None, "shard"),
            P(None, None, "shard"),
            P(None, "shard", None),
            P(None, "shard"),
            P(None, "shard", None),
            P(None, "shard"),
            P(None, "shard", None),
            P(None, "shard"),
            P(None, "shard", None),
            P(None, "shard"),
        ),
        check_vma=False,
    )
```

profile of v0, /device:TPU:0, one launch (start us, length us, event | category | flops | bytes accessed | tf_op | source)
XLA Modules:
  0.0 1638.9 jit_solution(7183254378653592078)
XLA Ops:
  14.3 21.5 %all-reduce.15 = (bf16[768]{0:T(1024)(128)(2,1)}, bf16[2304]{0:T(1024)(128)(2,1)S(1)}, bf16[768]{0:T(1024)(128)(2,1)}, bf16[2304]{0:T(1024)(128)(2,1)S(1)}) all-reduce(bf16[768]{0:T(1024)(128)(2,1)S(1)} %dynamic-update-slice.2, bf16[2304]{0:T(1024)(128)(2,1)S(1)} %dynamic-update-slice, ...), channel_id=11, replica_groups=mesh['rep'=8,'shard'=4] {'shard'}, use_global_device_ids=true, to_apply=%add.2 | all-reduce | flops 6144 | bytes 24576
  55.1 18.1 %all-gather.1 = bf16[1,2,768]{1,0,2:T(2,128)(2,1)S(1)} all-gather(bf16[1,2,192]{1,0,2:T(2,128)(2,1)S(1)} %copy.116), channel_id=3, replica_groups=mesh['rep'=8,'shard'=4] {'shard'}, dimensions={2}, use_global_device_ids=true | all-gather | bytes 3840 | tf_op jit(solution)/shard_map/all_gather | solution.py:205
  186.3 77.5 %all-gather.45.cloned.1.call-done = bf16[1,768,3072]{2,1,0:T(8,128)(2,1)} async-done(((bf16[1,192,3072]{2,1,0:T(8,128)(2,1)}), bf16[1,768,3072]{2,1,0:T(8,128)(2,1)}) %all-gather.45.cloned.1.call-update) | async-done | bytes 4718608 | tf_op jit(solution)/shard_map/all_gather | solution.py:210
  272.8 80.9 %all-gather.47.cloned.1.call-done = bf16[1,3072,768]{2,1,0:T(8,128)(2,1)} async-done(((bf16[1,768,768]{2,1,0:T(8,128)(2,1)}), bf16[1,3072,768]{2,1,0:T(8,128)(2,1)}) %all-gather.47.cloned.1.call-update) | async-done | bytes 4718608 | tf_op jit(solution)/shard_map/all_gather | solution.py:212
  357.1 26.9 %all-gather.43.cloned.1.call-done = bf16[1,768,768]{2,1,0:T(8,128)(2,1)} async-done(((bf16[1,192,768]{2,1,0:T(8,128)(2,1)}), bf16[1,768,768]{2,1,0:T(8,128)(2,1)}) %all-gather.43.cloned.1.call-update) | async-done | bytes 1179664 | tf_op jit(solution)/shard_map/all_gather | solution.py:208
  386.1 68.6 %all-gather.49.cloned.1.call-done = bf16[1,768,2304]{2,1,0:T(8,128)(2,1)} async-done(((bf16[1,192,2304]{2,1,0:T(8,128)(2,1)}), bf16[1,768,2304]{2,1,0:T(8,128)(2,1)}) %all-gather.49.cloned.1.call-update) | async-done | bytes 3538960 | tf_op jit(solution)/shard_map/all_gather | solution.py:206
  489.2 27.9 %all-gather.39.cloned.1.call-done = bf16[768,768]{1,0:T(8,128)(2,1)} async-done(((bf16[192,768]{1,0:T(8,128)(2,1)}), bf16[768,768]{1,0:T(8,128)(2,1)}) %all-gather.39.cloned.1.call-update) | async-done | bytes 1179664 | tf_op jit(solution)/shard_map/all_gather | solution.py:250
  518.9 29.8 %all-gather.37.cloned.1.call-done = bf16[768,768]{1,0:T(8,128)(2,1)} async-done(((bf16[192,768]{1,0:T(8,128)(2,1)}), bf16[768,768]{1,0:T(8,128)(2,1)}) %all-gather.37.cloned.1.call-update) | async-done | bytes 1179664 | tf_op jit(solution)/shard_map/all_gather | solution.py:251
  586.0 53.5 %all-gather.53.cloned.1.call-done = bf16[1,768,3072]{2,1,0:T(8,128)(2,1)} async-done(((bf16[1,192,3072]{2,1,0:T(8,128)(2,1)}), bf16[1,768,3072]{2,1,0:T(8,128)(2,1)}) %all-gather.53.cloned.1.call-update) | async-done | bytes 4718608 | tf_op jit(solution)/shard_map/all_gather | solution.py:210
  649.1 79.8 %all-gather.55.cloned.1.call-done = bf16[1,3072,768]{2,1,0:T(8,128)(2,1)} async-done(((bf16[1,768,768]{2,1,0:T(8,128)(2,1)}), bf16[1,3072,768]{2,1,0:T(8,128)(2,1)}) %all-gather.55.cloned.1.call-update) | async-done | bytes 4718608 | tf_op jit(solution)/shard_map/all_gather | solution.py:212
  739.1 19.8 %reduce-scatter.49.cloned.1.call-done = bf16[192,768]{1,0:T(8,128)(2,1)} async-done(((bf16[768,768]{1,0:T(8,128)(2,1)}), bf16[192,768]{1,0:T(8,128)(2,1)}) %reduce-scatter.49.cloned.1.call-update) | async-done | bytes 294928
  760.4 28.6 %reduce-scatter.51.cloned.1.call-done = bf16[192,768]{1,0:T(8,128)(2,1)} async-done(((bf16[768,768]{1,0:T(8,128)(2,1)}), bf16[192,768]{1,0:T(8,128)(2,1)}) %reduce-scatter.51.cloned.1.call-update) | async-done | bytes 294928
  844.4 26.8 %reduce-scatter.55.cloned.1.call-done = bf16[192,768]{1,0:T(8,128)(2,1)} async-done(((bf16[768,768]{1,0:T(8,128)(2,1)}), bf16[192,768]{1,0:T(8,128)(2,1)}) %reduce-scatter.55.cloned.1.call-update) | async-done | bytes 294928
  907.1 24.3 %reduce-scatter.37.cloned.1.call-done = bf16[192,768]{1,0:T(8,128)(2,1)} async-done(((bf16[768,768]{1,0:T(8,128)(2,1)}), bf16[192,768]{1,0:T(8,128)(2,1)}) %reduce-scatter.37.cloned.1.call-update) | async-done | bytes 294928 | tf_op jit(solution)/shard_map/reduce_scatter | solution.py:411
  931.4 86.9 %reduce-scatter.43.cloned.1.call-done = bf16[192,3072]{1,0:T(8,128)(2,1)} async-done(((bf16[768,3072]{1,0:T(8,128)(2,1)}), bf16[192,3072]{1,0:T(8,128)(2,1)}) %reduce-scatter.43.cloned.1.call-update) | async-done | bytes 1179664 | tf_op jit(solution)/shard_map/reduce_scatter | solution.py:417
  1018.3 88.0 %reduce-scatter.47.cloned.1.call-done = bf16[768,768]{1,0:T(8,128)(2,1)} async-done(((bf16[3072,768]{1,0:T(8,128)(2,1)}), bf16[768,768]{1,0:T(8,128)(2,1)}) %reduce-scatter.47.cloned.1.call-update) | async-done | bytes 1179664 | tf_op jit(solution)/shard_map/reduce_scatter | solution.py:423
  1106.3 69.2 %reduce-scatter.35.cloned.1.call-done = bf16[192,2304]{1,0:T(8,128)(2,1)} async-done(((bf16[768,2304]{1,0:T(8,128)(2,1)}), bf16[192,2304]{1,0:T(8,128)(2,1)}) %reduce-scatter.35.cloned.1.call-update) | async-done | bytes 884752 | tf_op jit(solution)/shard_map/reduce_scatter | solution.py:405
  1175.5 69.6 %reduce-scatter.33.cloned.1.call-done = bf16[192,2304]{1,0:T(8,128)(2,1)} async-done(((bf16[768,2304]{1,0:T(8,128)(2,1)}), bf16[192,2304]{1,0:T(8,128)(2,1)}) %reduce-scatter.33.cloned.1.call-update) | async-done | bytes 884752 | tf_op jit(solution)/shard_map/reduce_scatter | solution.py:405
  1245.1 88.4 %reduce-scatter.41.cloned.1.call-done = bf16[192,3072]{1,0:T(8,128)(2,1)} async-done(((bf16[768,3072]{1,0:T(8,128)(2,1)}), bf16[192,3072]{1,0:T(8,128)(2,1)}) %reduce-scatter.41.cloned.1.call-update) | async-done | bytes 1179664 | tf_op jit(solution)/shard_map/reduce_scatter | solution.py:417
  1333.5 88.0 %reduce-scatter.45.cloned.1.call-done = bf16[768,768]{1,0:T(8,128)(2,1)} async-done(((bf16[3072,768]{1,0:T(8,128)(2,1)}), bf16[768,768]{1,0:T(8,128)(2,1)}) %reduce-scatter.45.cloned.1.call-update) | async-done | bytes 1179664 | tf_op jit(solution)/shard_map/reduce_scatter | solution.py:423
  1425.6 18.1 %reduce-scatter.63.cloned.1.call-done = bf16[192,2]{1,0:T(8,128)(2,1)} async-done(((bf16[768,2]{1,0:T(8,128)(2,1)}), bf16[192,2]{1,0:T(8,128)(2,1)}) %reduce-scatter.63.cloned.1.call-update) | async-done | bytes 784
  1444.5 18.9 %reduce-scatter.59.cloned.1.call-done = bf16[192,2]{1,0:T(8,128)(2,1)} async-done(((bf16[768,2]{1,0:T(8,128)(2,1)}), bf16[192,2]{1,0:T(8,128)(2,1)}) %reduce-scatter.59.cloned.1.call-update) | async-done | bytes 784
  1504.8 23.3 %all-reduce.12 = (bf16[1,2,192]{2,1,0:T(2,128)(2,1)S(1)}, bf16[1,2,192]{2,1,0:T(2,128)(2,1)S(1)}, bf16[1,2,192]{2,1,0:T(2,128)(2,1)S(1)}, bf16[1,2,192]{2,1,0:T(...) all-reduce(bf16[1,2,192]{2,1,0:T(2,128)(2,1)S(1)} %bitcast.260, ...), channel_id=1, replica_groups=mesh['rep'=8,'shard'=4] {'rep'}, use_global_device_ids=true, to_apply=%region_32.33 | all-reduce | flops 4608 | bytes 18432 | tf_op jit(solution)/shard_map/psum | solution.py:431
  1530.5 90.2 %all-reduce.18.cloned.1.call-done = (bf16[1,192,2304]{2,1,0:T(8,128)(2,1)}, bf16[1,192,2304]{2,1,0:T(8,128)(2,1)}, bf16[1,192,768]{2,1,0:T(8,128)(2,1)}, bf16[1,...) async-done(((bf16[1,192,2304]{2,1,0:T(8,128)(2,1)}, ...) | async-done | bytes 7077904 | tf_op jit(solution)/shard_map/psum | solution.py:433
  (523 shorter events, 394.6 us)
Async XLA Ops:
  10.2 161.5 %all-gather.35.cloned.1.call-start = ((), (), s32[]{:S(2)}) async-start(), calls=%async_computation.17 | async-start | bytes 1474560 | tf_op jit(solution)/shard_map/all_gather | solution.py:250
  103.6 160.2 %all-gather.45.cloned.1.call-start = ((), (), s32[]{:S(2)}) async-start(), calls=%async_computation.30 | async-start | bytes 5898240 | tf_op jit(solution)/shard_map/all_gather | solution.py:210
  107.0 246.7 %all-gather.47.cloned.1.call-start = ((), (), s32[]{:S(2)}) async-start(), calls=%async_computation.31 | async-start | bytes 5898240 | tf_op jit(solution)/shard_map/all_gather | solution.py:212
  108.7 275.4 %all-gather.43.cloned.1.call-start = ((), (), s32[]{:S(2)}) async-start(), calls=%async_computation.29 | async-start | bytes 1474560 | tf_op jit(solution)/shard_map/all_gather | solution.py:208
  109.6 345.1 %all-gather.49.cloned.1.call-start = ((), (), s32[]{:S(2)}) async-start(), calls=%async_computation.32 | async-start | bytes 4423680 | tf_op jit(solution)/shard_map/all_gather | solution.py:206
  110.3 375.0 %all-gather.51.cloned.1.call-start = ((), (), s32[]{:S(2)}) async-start(), calls=%async_computation.33 | async-start | bytes 1474560 | tf_op jit(solution)/shard_map/all_gather | solution.py:208
  111.1 406.0 %all-gather.39.cloned.1.call-start = ((), (), s32[]{:S(2)}) async-start(), calls=%async_computation.19 | async-start | bytes 1474560 | tf_op jit(solution)/shard_map/all_gather | solution.py:250
  468.3 171.2 %all-gather.53.cloned.1.call-start = ((), (), s32[]{:S(2)}) async-start(), calls=%async_computation.34 | async-start | bytes 5898240 | tf_op jit(solution)/shard_map/all_gather | solution.py:210
  469.0 259.9 %all-gather.55.cloned.1.call-start = ((), (), s32[]{:S(2)}) async-start(), calls=%async_computation.35 | async-start | bytes 5898240 | tf_op jit(solution)/shard_map/all_gather | solution.py:212
  469.6 289.3 %reduce-scatter.49.cloned.1.call-start = ((), (), s32[]{:S(2)}) async-start(), calls=%async_computation.36 | async-start | bytes 1474560
  565.9 223.0 %reduce-scatter.51.cloned.1.call-start = ((), (), s32[]{:S(2)}) async-start(), calls=%async_computation.37 | async-start | bytes 1474560
  585.9 255.6 %reduce-scatter.53.cloned.1.call-start = ((), (), s32[]{:S(2)}) async-start(), calls=%async_computation.38 | async-start | bytes 1474560
  821.4 110.1 %reduce-scatter.37.cloned.1.call-start = ((), (), s32[]{:S(2)}) async-start(), calls=%async_computation.22 | async-start | bytes 1474560 | tf_op jit(solution)/shard_map/reduce_scatter | solution.py:411
  822.9 195.4 %reduce-scatter.43.cloned.1.call-start = ((), (), s32[]{:S(2)}) async-start(), calls=%async_computation.25 | async-start | bytes 5898240 | tf_op jit(solution)/shard_map/reduce_scatter | solution.py:417
  826.8 279.5 %reduce-scatter.47.cloned.1.call-start = ((), (), s32[]{:S(2)}) async-start(), calls=%async_computation.27 | async-start | bytes 5898240 | tf_op jit(solution)/shard_map/reduce_scatter | solution.py:423
  831.7 343.8 %reduce-scatter.35.cloned.1.call-start = ((), (), s32[]{:S(2)}) async-start(), calls=%async_computation.21 | async-start | bytes 4423680 | tf_op jit(solution)/shard_map/reduce_scatter | solution.py:405
  836.1 409.0 %reduce-scatter.33.cloned.1.call-start = ((), (), s32[]{:S(2)}) async-start(), calls=%async_computation.20 | async-start | bytes 4423680 | tf_op jit(solution)/shard_map/reduce_scatter | solution.py:405
  878.8 454.7 %reduce-scatter.41.cloned.1.call-start = ((), (), s32[]{:S(2)}) async-start(), calls=%async_computation.24 | async-start | bytes 5898240 | tf_op jit(solution)/shard_map/reduce_scatter | solution.py:417
  889.0 532.5 %reduce-scatter.45.cloned.1.call-start = ((), (), s32[]{:S(2)}) async-start(), calls=%async_computation.26 | async-start | bytes 5898240 | tf_op jit(solution)/shard_map/reduce_scatter | solution.py:423
  893.9 549.7 %reduce-scatter.63.cloned.1.call-start = ((), (), s32[]{:S(2)}) async-start(), calls=%async_computation.43 | async-start | bytes 245760
  895.5 568.0 %reduce-scatter.59.cloned.1.call-start = ((), (), s32[]{:S(2)}) async-start(), calls=%async_computation.41 | async-start | bytes 245760
  896.4 593.7 %reduce-scatter.61.cloned.1.call-start = ((), (), s32[]{:S(2)}) async-start(), calls=%async_computation.42 | async-start | bytes 245760
  905.8 598.0 %reduce-scatter.57.cloned.1.call-start = ((), (), s32[]{:S(2)}) async-start(), calls=%async_computation.40 | async-start | bytes 245760
  906.8 713.9 %all-reduce.18.cloned.1.call-start = ((), (), s32[]{:S(2)}) async-start(), calls=%async_computation.44 | async-start | bytes 14155776 | tf_op jit(solution)/shard_map/psum | solution.py:433
  (129 other events, 4356.5 us)
Sparse Core Ops, SparseCore 0:
  10.3 85.3 all-gather.40
  102.9 33.1 all-gather.34
  138.2 34.8 all-gather.32
  175.1 88.6 all-gather.44
  265.7 87.8 all-gather.46
  355.1 28.8 all-gather.42
  385.6 69.0 all-gather.48
  456.3 29.0 all-gather.50
  487.5 29.5 all-gather.38
  519.1 29.5 all-gather.36
  550.8 88.6 all-gather.52
  640.9 87.9 all-gather.54
  761.0 27.8 reduce-scatter.50
  813.2 27.8 reduce-scatter.52
  843.3 27.8 reduce-scatter.54
  873.4 27.8 reduce-scatter.38
  903.5 27.8 reduce-scatter.36
  934.3 83.9 reduce-scatter.42
  1020.4 85.7 reduce-scatter.46
  1108.6 66.8 reduce-scatter.34
  1178.4 66.6 reduce-scatter.32
  1248.0 85.5 reduce-scatter.40
  1335.7 85.7 reduce-scatter.44
  1508.0 112.6 all-reduce.17
  (5 shorter events, 100.1 us)
where the time goes:
time: 1650 us; the launch traced here: 1640 us
  waiting for transfers between devices  1200 us (73%)
  blocking collectives  159 us (10%)
  matrix products  131 us (8%)
  local copies, waits for them, and re-layouts  69.4 us (4%)
  other arithmetic  53.2 us (3%)
  between operations  19.7 us (1%)
    reduce_scatter x2, waiting for transfers between devices, per_device(): lax.psum_scatter(grad_w_back.astype(jnp.bfloat16), 'shard', scatter_dimen...  176 us
    reduce_scatter x2, waiting for transfers between devices, per_device(): lax.psum_scatter(grad_w_hidden.astype(jnp.bfloat16), 'shard', scatter_dim...  175 us
    all_gather x2, waiting for transfers between devices, per_device(): lax.all_gather(w_down[layer_index], 'shard', axis=0, tiled=True)  161 us
    reduce_scatter x2, waiting for transfers between devices, per_device(): lax.psum_scatter(grad_w_mixed.astype(jnp.bfloat16), 'shard', scatter_dime...  139 us
    all_gather x2, waiting for transfers between devices, per_device(): lax.all_gather(w_up[layer_index], 'shard', axis=0, tiled=True)  131 us
    unnamed x37, waiting for transfers between devices  128 us
    psum x1, waiting for transfers between devices, per_device(): lax.psum(reduced[2].astype(jnp.bfloat16), 'rep').astype(jnp.float32)  90.2 us
    all_gather x2, waiting for transfers between devices, per_device(): lax.all_gather(w_qkv[layer_index], 'shard', axis=0, tiled=True)  80.8 us
  transfers between devices with their start and end apart: 29, of which 24 were waited for; matrix products, arithmetic and copies ran while one was open for 12% of the time, Pallas kernels for 0%

commit v1 on v0

--- a/solution.py
+++ b/solution.py
@@ -158,7 +158,7 @@
     return (grad_query, outputs[0].reshape(-1, HEADS * HEAD), outputs[1].reshape(-1, HEADS * HEAD))
 
 
-def per_device(
+def gathered_per_device(
     tokens,
     seq_len,
     norm_gain,
@@ -461,6 +461,246 @@
     )
 
 
+def by_heads(array):
+    heads = array.shape[1] // HEAD
+    return jnp.stack([array[:, h * HEAD : (h + 1) * HEAD] for h in range(heads)])
+
+
+def from_heads(array):
+    return jnp.concatenate([array[h] for h in range(array.shape[0])], axis=1)
+
+
+def rotary_lanes(places, width):
+    half = ROT // 2
+    lane = jnp.arange(width, dtype=jnp.int32) % HEAD
+    inverse = jnp.exp((lane % half).astype(jnp.float32) * (-2.0 * math.log(10000.0) / ROT))
+    angles = places.astype(jnp.float32)[:, None] * inverse[None, :]
+    cosine, sine = jnp.cos(angles), jnp.sin(angles)
+    keep = jnp.where(lane < ROT, cosine, 1.0)
+    from_right = jnp.where(lane < half, -sine, 0.0)
+    from_left = jnp.where((lane >= half) & (lane < ROT), sine, 0.0)
+    return (keep, from_right, from_left)
+
+
+def rotate_lanes(field, tables, sign):
+    half = ROT // 2
+    keep, from_right, from_left = tables
+    turned = jnp.roll(field, -half, axis=1) * from_right + jnp.roll(field, half, axis=1) * from_left
+    return field * keep + sign * turned
+
+
+def dot32(left, right):
+    return jnp.dot(left, right, preferred_element_type=jnp.float32)
+
+
+def normalize(rows):
+    center = rows - jnp.mean(rows, axis=-1, keepdims=True)
+    scale = lax.rsqrt(jnp.mean(center * center, axis=-1, keepdims=True) + EPSILON)
+    return (center * scale, scale)
+
+
+def norm_back(grad, unit, scale):
+    level = jnp.mean(grad, axis=-1, keepdims=True)
+    along = jnp.mean(grad * unit, axis=-1, keepdims=True)
+    return scale * (grad - level - unit * along)
+
+
+def split_per_device(
+    tokens,
+    seq_len,
+    norm_gain,
+    norm_bias,
+    w_qkv,
+    b_qkv,
+    w_out,
+    b_out,
+    w_up,
+    b_up,
+    w_down,
+    b_down,
+    cotangent,
+):
+    shards = lax.axis_size("shard")
+    rank = lax.axis_index("shard")
+    rows, width = tokens.shape
+    part = width // shards
+    units = w_up.shape[2] // shards
+    total = rows * shards
+    f32 = jnp.float32
+    bf16 = jnp.bfloat16
+    score_scale = 1.0 / math.sqrt(HEAD)
+
+    tokens_all = lax.all_gather(tokens, "shard", axis=0, tiled=True)
+    small = [norm_gain, norm_bias, b_qkv, b_out, b_down]
+    packed = lax.all_gather(jnp.concatenate([v.reshape(-1) for v in small]), "shard", axis=0)
+    whole = []
+    at = 0
+    for v in small:
+        piece = packed[:, at : at + v.size].reshape((shards,) + v.shape)
+        whole.append(jnp.moveaxis(piece, 0, -2).reshape(v.shape[:-1] + (-1,)).astype(f32))
+        at += v.size
+    gains, shifts, bias_qkv, bias_out, bias_down = whole
+    bias_qkv = lax.dynamic_slice_in_dim(
+        bias_qkv.reshape(LAYERS, 3, width), rank * part, part, axis=2
+    ).reshape(LAYERS, 3 * part)
+    bias_up = b_up.astype(f32)
+
+    columns = []
+    for l in range(LAYERS):
+        up = w_up[l].reshape(part, shards, units).transpose(1, 0, 2)
+        qkv = w_qkv[l].reshape(part, 3, shards, part).transpose(2, 0, 1, 3)
+        both = jnp.concatenate([up, qkv.reshape(shards, part, 3 * part)], axis=2)
+        both = lax.all_to_all(both, "shard", 0, 0).reshape(width, units + 3 * part)
+        columns.append((both[:, :units], both[:, units:]))
+    cotangent_all = lax.all_gather(cotangent, "shard", axis=0, tiled=True)
+
+    doc_ids, places = sequence_layout(seq_len[0], total)
+    tables = rotary_lanes(places, 2 * part)
+    order = jnp.arange(total, dtype=jnp.int32)
+    allowed = (doc_ids[:, None] == doc_ids[None, :]) & (order[:, None] >= order[None, :])
+
+    resid = tokens_all.astype(f32)
+    stored = []
+    output = None
+    for l in range(LAYERS):
+        col_up, col_qkv = columns[l]
+        unit, scale = normalize(resid)
+        first = (unit * gains[l, 0] + shifts[l, 0]).astype(bf16)
+        second = (unit * gains[l, 1] + shifts[l, 1]).astype(bf16)
+        mixed = dot32(first, col_qkv) + bias_qkv[l]
+        turned = rotate_lanes(mixed[:, : 2 * part], tables, 1.0).astype(bf16)
+        query, key = by_heads(turned[:, :part]), by_heads(turned[:, part:])
+        value = by_heads(mixed[:, 2 * part :].astype(bf16))
+        scores = jnp.einsum("hqd,hkd->hqk", query, key, preferred_element_type=f32) * score_scale
+        scores = jnp.where(allowed[None], scores, MASKED)
+        raised = jnp.exp(scores - jnp.max(scores, axis=-1, keepdims=True))
+        probs = raised / jnp.sum(raised, axis=-1, keepdims=True)
+        probs16 = probs.astype(bf16)
+        attended = from_heads(
+            jnp.einsum("hqk,hkd->hqd", probs16, value, preferred_element_type=f32).astype(bf16)
+        )
+        hidden = dot32(second, col_up) + bias_up[l]
+        active = jax.nn.gelu(hidden, approximate=False).astype(bf16)
+        branch = (dot32(attended, w_out[l]) + dot32(active, w_down[l])).astype(bf16)
+        bias = bias_out[l] + bias_down[l]
+        stored.append((unit, scale, first, second, query, key, value, probs, attended, hidden, active))
+        if l < LAYERS - 1:
+            resid = resid + lax.psum(branch, "shard").astype(f32) + bias
+        else:
+            own = lax.dynamic_slice_in_dim(resid, rank * rows, rows)
+            summed = lax.psum_scatter(branch, "shard", scatter_dimension=0, tiled=True)
+            output = own + summed.astype(f32) + bias
+
+    gradient = cotangent_all
+    grad_tokens = None
+    weight_grads = [None] * LAYERS
+    vectors = [None] * LAYERS
+    for l in range(LAYERS - 1, -1, -1):
+        unit, scale, first, second, query, key, value, probs, attended, hidden, active = stored[l]
+        col_up, col_qkv = columns[l]
+        grad16 = gradient.astype(bf16)
+        grad_bias = jnp.sum(grad16, axis=0, dtype=f32)
+        grad_down = dot32(active.T, grad16).astype(bf16)
+        grad_out = dot32(attended.T, grad16).astype(bf16)
+        grad_active = dot32(grad16, w_down[l].T)
+        _, pull = jax.vjp(lambda v: jax.nn.gelu(v, approximate=False), hidden)
+        grad_hidden = pull(grad_active)[0].astype(bf16)
+        grad_up = dot32(second.T, grad_hidden).astype(bf16)
+        grad_b_up = jnp.sum(grad_hidden, axis=0, dtype=f32)
+        back_second = dot32(grad_hidden, col_up.T)
+
+        grad_att = by_heads(dot32(grad16, w_out[l].T).astype(bf16))
+        grad_probs = jnp.einsum("hqd,hkd->hqk", grad_att, value, preferred_element_type=f32)
+        delta = jnp.sum(probs * grad_probs, axis=-1, keepdims=True)
+        grad_scores = (probs * (grad_probs - delta)).astype(bf16)
+        grad_query = jnp.einsum("hqk,hkd->hqd", grad_scores, key, preferred_element_type=f32)
+        grad_key = jnp.einsum("hqk,hqd->hkd", grad_scores, query, preferred_element_type=f32)
+        grad_value = jnp.einsum(
+            "hqk,hqd->hkd", probs.astype(bf16), grad_att, preferred_element_type=f32
+        )
+        turned = jnp.concatenate([from_heads(grad_query), from_heads(grad_key)], axis=1)
+        turned = rotate_lanes(turned * score_scale, tables, -1.0)
+        grad_mixed = jnp.concatenate([turned, from_heads(grad_value)], axis=1).astype(bf16)
+        grad_b_mixed = jnp.sum(grad_mixed, axis=0, dtype=f32)
+        grad_qkv = dot32(first.T, grad_mixed).astype(bf16)
+        back_first = dot32(grad_mixed, col_qkv.T)
+
+        combined = (back_first * gains[l, 0] + back_second * gains[l, 1]).astype(bf16)
+        if l > 0:
+            summed = lax.psum(combined, "shard").astype(f32)
+            gradient = gradient + norm_back(summed, unit, scale)
+        else:
+            summed = lax.psum_scatter(combined, "shard", scatter_dimension=0, tiled=True)
+            own = [
+                lax.dynamic_slice_in_dim(v, rank * rows, rows) for v in (gradient, unit, scale)
+            ]
+            grad_tokens = own[0] + norm_back(summed.astype(f32), own[1], own[2])
+
+        moved = jnp.concatenate([grad_up, grad_qkv], axis=1)
+        moved = lax.all_to_all(moved.reshape(shards, part, units + 3 * part), "shard", 0, 0)
+        weight_grads[l] = lax.psum((moved, grad_out, grad_down), "rep")
+
+        def placed(vector, start, size):
+            return lax.dynamic_update_slice_in_dim(jnp.zeros((size,), f32), vector, start, 0)
+
+        own_bias = lax.dynamic_slice_in_dim(grad_bias, rank * part, part)
+        vectors[l] = jnp.concatenate(
+            [
+                jnp.sum(back_first * unit, axis=0),
+                jnp.sum(back_second * unit, axis=0),
+                jnp.sum(back_first, axis=0),
+                jnp.sum(back_second, axis=0),
+                *[
+                    placed(grad_b_mixed[i * part : (i + 1) * part], rank * part, width)
+                    for i in range(3)
+                ],
+                placed(own_bias, rank * part, width),
+                placed(grad_b_up, rank * units, units * shards),
+            ]
+        )
+
+    small_grads = lax.psum(jnp.stack(vectors), ("rep", "shard"))
+    norm_grads = lax.dynamic_slice_in_dim(
+        small_grads[:, : 4 * width].reshape(LAYERS, 2, 2, width), rank * part, part, axis=3
+    )
+    g_b_qkv = lax.dynamic_slice_in_dim(
+        small_grads[:, 4 * width : 7 * width], rank * 3 * part, 3 * part, axis=1
+    )
+    g_b_out = lax.dynamic_slice_in_dim(
+        small_grads[:, 7 * width : 8 * width], rank * part, part, axis=1
+    )
+    g_b_up = lax.dynamic_slice_in_dim(small_grads[:, 8 * width :], rank * units, units, axis=1)
+
+    g_qkv, g_up, g_out, g_down = [], [], [], []
+    for l in range(LAYERS):
+        moved, grad_out, grad_down = weight_grads[l]
+        g_up.append(moved[:, :, :units].transpose(1, 0, 2).reshape(part, -1).astype(f32))
+        qkv = moved[:, :, units:].reshape(shards, part, 3, part)
+        g_qkv.append(qkv.transpose(1, 2, 0, 3).reshape(part, -1).astype(f32))
+        g_out.append(grad_out.astype(f32))
+        g_down.append(grad_down.astype(f32))
+    return (
+        output,
+        grad_tokens,
+        norm_grads[:, 0],
+        norm_grads[:, 1],
+        jnp.stack(g_qkv),
+        g_b_qkv,
+        jnp.stack(g_out),
+        g_b_out,
+        jnp.stack(g_up),
+        g_b_up,
+        jnp.stack(g_down),
+        g_b_out,
+    )
+
+
+def per_device(*args):
+    if HEADS % lax.axis_size("shard") == 0:
+        return split_per_device(*args)
+    return gathered_per_device(*args)
+
+
 def solution(mesh):
     return jax.shard_map(
         per_device,

time: 1650 us -> 826 us (0.50)
  waiting for transfers between devices: 1200 us -> 418 us
  blocking collectives: 159 us -> 95 us
  matrix products: 131 us -> 108 us
  starting transfers between devices: 1.66 us -> 20.8 us
  other arithmetic: 53.2 us -> 72.3 us
  local copies, waits for them, and re-layouts: 69.4 us -> 87.3 us
    all_gather x12 -> x2, waiting for transfers between devices: 472 us -> 0.01 us  [the longest x1 0.01 us: split_per_device(): tokens_all = lax.all_gather(tokens, 'shard', axis=0, tiled=True)]
    reduce_scatter x8 -> x2, waiting for transfers between devices: 514 us -> 57.4 us  [the longest x1 29 us: split_per_device(): summed = lax.psum_scatter(branch, 'shard', scatter_dimension=0, tiled=True)]
    psum x1 -> x4, waiting for transfers between devices: 90.2 us -> 317 us  [the longest x1 116 us: split_per_device(): weight_grads[l] = lax.psum((moved, grad_out, grad_down), 'rep')]
    unnamed x37 -> x8, waiting for transfers between devices: 128 us -> 2.18 us
    all_to_all x0 -> x4, waiting for transfers between devices: none -> 40.6 us  [the longest x2 40.6 us: split_per_device(): lax.all_to_all(moved.reshape(shards, part, units + 3 * part), 'shard', 0, 0)]
    unnamed x2 -> x0, blocking collectives: 37.9 us -> none
    dot_general x38 -> x34, matrix products: 131 us -> 94.9 us  [the longest x24 67.6 us: dot32(): return jnp.dot(left, right, preferred_element_type=jnp.float32)]
    psum x1 -> x0, blocking collectives: 23.3 us -> none  [per_device(): lax.psum(reduced[0].astype(jnp.bfloat16), 'rep').astype(jnp.float32)]
  transfers between devices with their start and end apart: 29 -> 12, of which waited for: 24 -> 7; matrix products, arithmetic and copies ran while one was open for 12% -> 20% of each run, Pallas kernels for 0% -> 0%
where the time goes in v1:
time: 826 us; the launch traced here: 817 us
  waiting for transfers between devices  418 us (51%)
  matrix products  108 us (13%)
  blocking collectives  95 us (12%)
  local copies, waits for them, and re-layouts  87.3 us (11%)
  other arithmetic  72.3 us (9%)
  starting transfers between devices  20.8 us (3%)
  between operations  16.4 us (2%)
    psum x1, waiting for transfers between devices, split_per_device(): weight_grads[l] = lax.psum((moved, grad_out, grad_down), 'rep')  116 us
    all_gather x1, blocking collectives, split_per_device(): lax.all_gather(jnp.concatenate([v.reshape(-1) for v in small]), 'shard',...  95 us
    psum x1, waiting for transfers between devices, split_per_device(): small_grads = lax.psum(jnp.stack(vectors), ('rep', 'shard'))  77.5 us
    dot_general x24, matrix products, dot32(): return jnp.dot(left, right, preferred_element_type=jnp.float32)  67.6 us
    psum x1, waiting for transfers between devices, split_per_device(): summed = lax.psum(combined, 'shard').astype(f32)  64.5 us
    psum x1, waiting for transfers between devices, split_per_device(): resid = resid + lax.psum(branch, 'shard').astype(f32) + bias  59.1 us
    all_to_all x2, waiting for transfers between devices, split_per_device(): lax.all_to_all(moved.reshape(shards, part, units + 3 * part), 'shard', 0, 0)  40.6 us
    reduce_scatter x1, waiting for transfers between devices, split_per_device(): summed = lax.psum_scatter(branch, 'shard', scatter_dimension=0, tiled=True)  29 us
  transfers between devices with their start and end apart: 12, of which 7 were waited for; matrix products, arithmetic and copies ran while one was open for 20% of the time, Pallas kernels for 0%

profile of v1, /device:TPU:0, one launch (start us, length us, event | category | flops | bytes accessed | tf_op | source)
XLA Modules:
  0.0 817.0 jit_solution(6979903316403788166)
XLA Ops:
  19.3 6.5 all-to-all-start
  27.9 95.0 %all-gather.1 = bf16[4,1,3456]{2,1,0:T(2,128)(2,1)S(1)} all-gather(bf16[1,1,3456]{2,1,0:T(2,128)(2,1)S(1)} %reshape.333), channel_id=2, replica_groups=mesh['rep'=8,'shard'=4] {'shard'}, dimensions={0}, use_global_device_ids=true | all-gather | bytes 34560 | tf_op jit(solution)/shard_map/all_gather | solution.py:535
  136.8 4.6 all-to-all-start.1
  144.4 5.4 fusion.65
  149.9 5.3 fusion.195
  159.1 8.9 %multiply_convert_fusion.3 = (bf16[768,768]{1,0:T(8,128)(2,1)S(1)}, f32[768,768]{1,0:T(8,128)}, f32[768,768]{1,0:T(8,128)}) fusion(f32[768]{0:T(1024)S(1)} %get-tuple-element.35, bf16[768,1344]{1,0:T(8,128)(2,1)} %bitcast.6, bf16[768,768]{1,0:T(8,128)(2,1)S(1)} %copy-done, f32[768]{0:T(1024)S(1)} %get-tuple-element.32, f32[768]{0:T(1024)S(1)} %get-tuple-element.146, ...), kind=kOutput, calls=%fused_computation.72 | convolution fusion | flops 948436992 | bytes 8272896 | tf_op jit(solution)/shard_map/dot_general | solution.py:493
  177.7 59.1 %all-reduce.6.cloned.1.call-done = bf16[768,768]{1,0:T(8,128)(2,1)} async-done(((bf16[768,768]{1,0:T(8,128)(2,1)}), bf16[768,768]{1,0:T(8,128)(2,1)}) %all-reduce.6.cloned.1.call-update) | async-done | bytes 1179664 | tf_op jit(solution)/shard_map/psum | solution.py:588
  242.0 5.3 fusion.68
  248.9 7.4 fusion.197
  256.3 7.5 multiply_reduce_fusion.1
  273.3 5.6 fusion.72
  284.4 8.4 %multiply_convert_fusion.2 = (bf16[768,768]{1,0:T(8,128)(2,1)}, f32[768,768]{1,0:T(8,128)S(1)}, f32[768,768]{1,0:T(8,128)S(1)}) fusion(f32[768]{0:T(1024)S(1)} %copy-done.105, bf16[768,1344]{1,0:T(8,128)(2,1)} %bitcast.27, f32[768]{0:T(1024)S(1)} %copy-done.101, f32[768]{0:T(1024)S(1)} %copy-done.65, f32[768]{0:T(1024)S(1)} %add_rsqrt_fusion, ...), kind=kOutput, calls=%fused_computation.55 | convolution fusion | flops 947847168 | bytes 9452544 | tf_op jit(solution)/shard_map/dot_general | solution.py:493
  297.5 4.2 add_convert_fusion.2
  309.2 4.5 all-to-all-start.3
  328.9 64.5 %all-reduce.8.cloned.1.call-done = bf16[768,768]{1,0:T(8,128)(2,1)} async-done(((bf16[768,768]{1,0:T(8,128)(2,1)}), bf16[768,768]{1,0:T(8,128)(2,1)}) %all-reduce.8.cloned.1.call-update) | async-done | bytes 1179664 | tf_op jit(solution)/shard_map/psum | solution.py:630
  393.4 4.2 multiply_reduce_fusion.2
  415.6 5.5 fusion.76
  426.8 4.7 fusion.176
  460.8 4.6 all-to-all-start.2
  475.4 40.6 %all-to-all-done.2 = bf16[4,192,1344]{2,1,0:T(8,128)(2,1)} async-done(((bf16[4,192,1344]{2,1,0:T(8,128)(2,1)}), bf16[4,192,1344]{2,1,0:T(8,128)(2,1)}, u32[]{:S(2)}, u32[]{:S(2)}) %all-to-all-start.2) | async-done | bytes 2064416 | tf_op jit(solution)/shard_map/all_to_all | solution.py:640
  516.8 77.5 %all-reduce.10.cloned.1.call-done = f32[2,9216]{1,0:T(2,128)} async-done(((f32[2,9216]{1,0:T(2,128)}), f32[2,9216]{1,0:T(2,128)}) %all-reduce.10.cloned.1.call-update) | async-done | bytes 73744 | tf_op jit(solution)/shard_map/psum | solution.py:662
  598.6 29.0 %reduce-scatter.3.cloned.1.call-done = bf16[192,768]{1,0:T(8,128)(2,1)} async-done(((bf16[768,768]{1,0:T(8,128)(2,1)}), bf16[192,768]{1,0:T(8,128)(2,1)}) %reduce-scatter.3.cloned.1.call-update) | async-done | bytes 294928 | tf_op jit(solution)/shard_map/reduce_scatter | solution.py:591
  629.4 28.4 %reduce-scatter.5.cloned.1.call-done = bf16[192,768]{1,0:T(8,128)(2,1)} async-done(((bf16[768,768]{1,0:T(8,128)(2,1)}), bf16[192,768]{1,0:T(8,128)(2,1)}) %reduce-scatter.5.cloned.1.call-update) | async-done | bytes 294928 | tf_op jit(solution)/shard_map/reduce_scatter | solution.py:633
  661.5 116.4 %all-reduce.12.cloned.1.call-done = (bf16[4,192,1344]{2,1,0:T(8,128)(2,1)}, bf16[4,192,1344]{2,1,0:T(8,128)(2,1)}, bf16[1,192,768]{2,1,0:T(8,128)(2,1)}, bf16[1,...) async-done(((bf16[4,192,1344]{2,1,0:T(8,128)(2,1)}, bf16[4,192,1344]{2,1,0:T(8,128)(2,1)}, bf16[1,192,768]{2,1,0:T(8,128)(2,1)}, ...) | async-done | bytes 7077904 | tf_op jit(solution)/shard_map/psum | solution.py:641
  (499 shorter events, 197.7 us)
Async XLA Ops:
  7.2 126.3 %all-gather.5.cloned.1.call-start = ((), (), s32[]{:S(2)}) async-start(), calls=%async_computation.6 | async-start | bytes 1474560 | tf_op jit(solution)/shard_map/all_gather | solution.py:533
  19.3 106.2 %copy-start.117 = (s32[1,8]{1,0:T(1,128)S(1)}, s32[1,8]{1,0:T(1,128)}, u32[]{:S(2)}) copy-start(s32[1,8]{1,0:T(1,128)} %param.14) | copy-start | bytes 100
  19.3 106.9 %copy-start.107 = (bf16[2,768]{1,0:T(2,128)(2,1)S(1)}, bf16[2,768]{1,0:T(2,128)(2,1)}, u32[]{:S(2)}) copy-start(bf16[2,768]{1,0:T(2,128)(2,1)} %param.22) | copy-start | bytes 9220
  19.3 106.9 %copy-start.5 = (bf16[1,192,2304]{2,1,0:T(8,128)(2,1)S(1)}, bf16[1,192,2304]{2,1,0:T(8,128)(2,1)}, u32[]{:S(2)}) copy-start(bf16[1,192,2304]{2,1,0:T(8,128)(2,1)} %get-tuple-element.69) | copy-start | bytes 2654212
  19.3 117.5 %all-to-all-start = ((bf16[4,192,1344]{2,1,0:T(8,128)(2,1)}), bf16[4,192,1344]{2,1,0:T(8,128)(2,1)}, u32[]{:S(2)}, u32[]{:S(2)}) async-start(bf16[4,192,1344]{2,1,0:T(8,128)(2,1)} %pad_maximum_fusion), calls=%async_computation | async-start | bytes 4325376 | tf_op jit(solution)/shard_map/all_to_all | solution.py:553
  25.8 147.7 %all-gather.7.cloned.1.call-start = ((), (), s32[]{:S(2)}) async-start(), calls=%async_computation.9 | async-start | bytes 2949120 | tf_op jit(solution)/shard_map/all_gather | solution.py:555
  130.1 14.3 %copy-start.78 = (pred[384]{0:T(512)(128)(4,1)}, pred[384]{0:T(512)(128)(4,1)S(1)}, u32[]{:S(2)}) copy-start(pred[384]{0:T(512)(128)(4,1)S(1)} %fusion.156) | copy-start | bytes 1156
  130.7 28.3 %copy-start.103 = (f32[768]{0:T(1024)}, f32[768]{0:T(1024)S(1)}, u32[]{:S(2)}) copy-start(f32[768]{0:T(1024)S(1)} %get-tuple-element.35) | copy-start | bytes 9220
  131.5 27.6 %copy-start.93 = (f32[768]{0:T(1024)}, f32[768]{0:T(1024)S(1)}, u32[]{:S(2)}) copy-start(f32[768]{0:T(1024)S(1)} %get-tuple-element.32) | copy-start | bytes 9220
  131.5 27.6 %copy-start.95 = (f32[768]{0:T(1024)}, f32[768]{0:T(1024)S(1)}, u32[]{:S(2)}) copy-start(f32[768]{0:T(1024)S(1)} %get-tuple-element.146) | copy-start | bytes 9220
  131.9 18.0 %copy-start.17 = (pred[768,768]{0,1:T(8,128)(4,1)}, pred[768,768]{0,1:T(8,128)(4,1)S(1)}, u32[]{:S(2)}) copy-start(pred[768,768]{0,1:T(8,128)(4,1)S(1)} %fusion.34) | copy-start | bytes 1769476
  135.0 24.1 %copy-start.67 = (f32[768]{0:T(1024)}, f32[768]{0:T(1024)S(1)}, u32[]{:S(2)}) copy-start(f32[768]{0:T(1024)S(1)} %broadcast_multiply_fusion.5) | copy-start | bytes 9220
  136.8 22.3 %copy-start.90 = (f32[768]{0:T(1024)}, f32[768]{0:T(1024)S(1)}, u32[]{:S(2)}) copy-start(f32[768]{0:T(1024)S(1)} %add_rsqrt_fusion.1) | copy-start | bytes 9220
  136.8 102.1 %all-to-all-start.1 = ((bf16[4,192,1344]{2,1,0:T(8,128)(2,1)}), bf16[4,192,1344]{2,1,0:T(8,128)(2,1)}, u32[]{:S(2)}, u32[]{:S(2)}) async-start(bf16[4,192,1344]{2,1,0:T(8,128)(2,1)} %pad_maximum_fusion.1), calls=%async_computation.1 | async-start | bytes 4325376 | tf_op jit(solution)/shard_map/all_to_all | solution.py:553
  141.4 95.3 %all-reduce.6.cloned.1.call-start = ((), (), s32[]{:S(2)}) async-start(), calls=%async_computation.7 | async-start | bytes 2359296 | tf_op jit(solution)/shard_map/psum | solution.py:588
  171.2 222.2 %all-reduce.8.cloned.1.call-start = ((), (), s32[]{:S(2)}) async-start(), calls=%async_computation.10 | async-start | bytes 2359296 | tf_op jit(solution)/shard_map/psum | solution.py:630
  281.4 16.1 %copy-start.1 = (f32[768,768]{1,0:T(8,128)}, f32[768,768]{1,0:T(8,128)S(1)}, u32[]{:S(2)}) copy-start(f32[768,768]{1,0:T(8,128)S(1)} %fusion.113) | copy-start | bytes 7077892
  309.2 151.6 %all-to-all-start.3 = ((bf16[4,192,1344]{2,1,0:T(8,128)(2,1)}), bf16[4,192,1344]{2,1,0:T(8,128)(2,1)}, u32[]{:S(2)}, u32[]{:S(2)}) async-start(bf16[4,192,1344]{2,1,0:T(8,128)(2,1)} %bitcast.228), calls=%async_computation.5 | async-start | bytes 4325376 | tf_op jit(solution)/shard_map/all_to_all | solution.py:640
  313.7 280.6 %all-reduce.10.cloned.1.call-start = ((), (), s32[]{:S(2)}) async-start(), calls=%async_computation.12 | async-start | bytes 147456 | tf_op jit(solution)/shard_map/psum | solution.py:662
  447.8 179.8 %reduce-scatter.3.cloned.1.call-start = ((), (), s32[]{:S(2)}) async-start(), calls=%async_computation.8 | async-start | bytes 1474560 | tf_op jit(solution)/shard_map/reduce_scatter | solution.py:591
  460.8 55.1 %all-to-all-start.2 = ((bf16[4,192,1344]{2,1,0:T(8,128)(2,1)}), bf16[4,192,1344]{2,1,0:T(8,128)(2,1)}, u32[]{:S(2)}, u32[]{:S(2)}) async-start(bf16[4,192,1344]{2,1,0:T(8,128)(2,1)} %bitcast.229), calls=%async_computation.4 | async-start | bytes 4325376 | tf_op jit(solution)/shard_map/all_to_all | solution.py:640
  465.4 192.4 %reduce-scatter.5.cloned.1.call-start = ((), (), s32[]{:S(2)}) async-start(), calls=%async_computation.11 | async-start | bytes 1474560 | tf_op jit(solution)/shard_map/reduce_scatter | solution.py:633
  466.2 311.7 %all-reduce.12.cloned.1.call-start = ((), (), s32[]{:S(2)}) async-start(), calls=%async_computation.13 | async-start | bytes 14548992 | tf_op jit(solution)/shard_map/psum | solution.py:641
  595.9 213.5 %copy-start.77 = (f32[2,192]{1,0:T(2,128)}, f32[2,192]{1,0:T(2,128)S(1)}, u32[]{:S(2)}) copy-start(f32[2,192]{1,0:T(2,128)S(1)} %constant_dynamic-slice_fusion.2) | copy-start | bytes 4612
  (119 other events, 442.9 us)
Sparse Core Ops, SparseCore 0:
  9.6 51.4 all-gather.4
  62.6 65.6 all-gather.6
  171.3 65.4 all-reduce.5
  301.8 91.5 all-reduce.7
  447.9 146.3 all-reduce.9
  596.5 31.0 reduce-scatter.2
  629.9 27.8 reduce-scatter.4
  663.0 114.8 all-reduce.11

commit v2 on v1

--- a/solution.py
+++ b/solution.py
@@ -552,7 +552,7 @@
         both = jnp.concatenate([up, qkv.reshape(shards, part, 3 * part)], axis=2)
         both = lax.all_to_all(both, "shard", 0, 0).reshape(width, units + 3 * part)
         columns.append((both[:, :units], both[:, units:]))
-    cotangent_all = lax.all_gather(cotangent, "shard", axis=0, tiled=True)
+    cotangent_all = None
 
     doc_ids, places = sequence_layout(seq_len[0], total)
     tables = rotary_lanes(places, 2 * part)
@@ -567,6 +567,9 @@
         unit, scale = normalize(resid)
         first = (unit * gains[l, 0] + shifts[l, 0]).astype(bf16)
         second = (unit * gains[l, 1] + shifts[l, 1]).astype(bf16)
+        if l == 0:
+            late, first = lax.optimization_barrier((cotangent.astype(bf16), first))
+            cotangent_all = lax.all_gather(late, "shard", axis=0, tiled=True).astype(f32)
         mixed = dot32(first, col_qkv) + bias_qkv[l]
         turned = rotate_lanes(mixed[:, : 2 * part], tables, 1.0).astype(bf16)
         query, key = by_heads(turned[:, :part]), by_heads(turned[:, part:])
@@ -592,6 +595,7 @@
             output = own + summed.astype(f32) + bias
 
     gradient = cotangent_all
+    own_gradient = cotangent
     grad_tokens = None
     weight_grads = [None] * LAYERS
     vectors = [None] * LAYERS
@@ -628,17 +632,23 @@
         combined = (back_first * gains[l, 0] + back_second * gains[l, 1]).astype(bf16)
         if l > 0:
             summed = lax.psum(combined, "shard").astype(f32)
-            gradient = gradient + norm_back(summed, unit, scale)
+            change = norm_back(summed, unit, scale)
+            gradient = gradient + change
+            own_gradient = own_gradient + lax.dynamic_slice_in_dim(change, rank * rows, rows)
         else:
             summed = lax.psum_scatter(combined, "shard", scatter_dimension=0, tiled=True)
-            own = [
-                lax.dynamic_slice_in_dim(v, rank * rows, rows) for v in (gradient, unit, scale)
-            ]
-            grad_tokens = own[0] + norm_back(summed.astype(f32), own[1], own[2])
+            own = [lax.dynamic_slice_in_dim(v, rank * rows, rows) for v in (unit, scale)]
+            grad_tokens = own_gradient + norm_back(summed.astype(f32), own[0], own[1])
 
         moved = jnp.concatenate([grad_up, grad_qkv], axis=1)
-        moved = lax.all_to_all(moved.reshape(shards, part, units + 3 * part), "shard", 0, 0)
-        weight_grads[l] = lax.psum((moved, grad_out, grad_down), "rep")
+        moved = moved.reshape(shards, part, units + 3 * part)
+        if l > 0:
+            moved, grad_out, grad_down = lax.psum((moved, grad_out, grad_down), "rep")
+            moved = lax.all_to_all(moved, "shard", 0, 0)
+            weight_grads[l] = (moved, grad_out, grad_down)
+        else:
+            moved = lax.all_to_all(moved, "shard", 0, 0)
+            weight_grads[l] = lax.psum((moved, grad_out, grad_down), "rep")
 
         def placed(vector, start, size):
             return lax.dynamic_update_slice_in_dim(jnp.zeros((size,), f32), vector, start, 0)

time: 826 us -> 827 us (level)
  blocking collectives: 95 us -> 67 us
  waiting for transfers between devices: 418 us -> 435 us
  local copies, waits for them, and re-layouts: 87.3 us -> 96.6 us
    psum x1, waiting for transfers between devices: 77.5 us -> 143 us  [split_per_device(): small_grads = lax.psum(jnp.stack(vectors), ('rep', 'shard'))]
    psum x1, waiting for transfers between devices: 116 us -> 86.9 us  [split_per_device(): moved, grad_out, grad_down = lax.psum((moved, grad_out, grad_down), 'rep')]
    all_gather x1, blocking collectives: 95 us -> 67 us  [split_per_device(): lax.all_gather(jnp.concatenate([v.reshape(-1) for v in small]), 'shard',...]
    psum x1, waiting for transfers between devices: 64.5 us -> 39.7 us  [split_per_device(): summed = lax.psum(combined, 'shard').astype(f32)]
    all_to_all x2, waiting for transfers between devices: 40.6 us -> 21.3 us  [split_per_device(): moved = lax.all_to_all(moved, 'shard', 0, 0)]
    all_gather x1, waiting for transfers between devices: 0.01 us -> 14.4 us  [split_per_device(): lax.all_gather(late, 'shard', axis=0, tiled=True).astype(f32)]
    unnamed x295 -> x309, local copies, waits for them, and re-layouts: 19.4 us -> 32.1 us
    psum x1, waiting for transfers between devices: 59.1 us -> 70.1 us  [split_per_device(): resid = resid + lax.psum(branch, 'shard').astype(f32) + bias]
  transfers between devices with their start and end apart: 12 -> 12, of which waited for: 7 -> 8; matrix products, arithmetic and copies ran while one was open for 20% -> 19% of each run, Pallas kernels for 0% -> 0%
where the time goes in v2:
time: 827 us; the launch traced here: 817 us
  waiting for transfers between devices  435 us (53%)
  matrix products  105 us (13%)
  local copies, waits for them, and re-layouts  96.6 us (12%)
  other arithmetic  75.2 us (9%)
  blocking collectives  67 us (8%)
  starting transfers between devices  21.1 us (3%)
  between operations  16.6 us (2%)
    psum x1, waiting for transfers between devices, split_per_device(): small_grads = lax.psum(jnp.stack(vectors), ('rep', 'shard'))  143 us
    psum x1, waiting for transfers between devices, split_per_device(): moved, grad_out, grad_down = lax.psum((moved, grad_out, grad_down), 'rep')  86.9 us
    psum x1, waiting for transfers between devices, split_per_device(): resid = resid + lax.psum(branch, 'shard').astype(f32) + bias  70.1 us
    dot_general x24, matrix products, dot32(): return jnp.dot(left, right, preferred_element_type=jnp.float32)  68.5 us
    all_gather x1, blocking collectives, split_per_device(): lax.all_gather(jnp.concatenate([v.reshape(-1) for v in small]), 'shard',...  67 us
    psum x1, waiting for transfers between devices, split_per_device(): summed = lax.psum(combined, 'shard').astype(f32)  39.7 us
    unnamed x309, local copies, waits for them, and re-layouts  32.1 us
    reduce_scatter x1, waiting for transfers between devices, split_per_device(): summed = lax.psum_scatter(branch, 'shard', scatter_dimension=0, tiled=True)  29.7 us
  transfers between devices with their start and end apart: 12, of which 8 were waited for; matrix products, arithmetic and copies ran while one was open for 19% of the time, Pallas kernels for 0%

profile of v2, /device:TPU:0, one launch (start us, length us, event | category | flops | bytes accessed | tf_op | source)
XLA Modules:
  0.0 817.2 jit_solution(12975987512527717180)
XLA Ops:
  19.3 6.5 all-to-all-start
  27.1 67.0 %all-gather.1 = bf16[4,1,3456]{2,1,0:T(2,128)(2,1)S(1)} all-gather(bf16[1,1,3456]{2,1,0:T(2,128)(2,1)S(1)} %reshape.333), channel_id=2, replica_groups=mesh['rep'=8,'shard'=4] {'shard'}, dimensions={0}, use_global_device_ids=true | all-gather | bytes 34560 | tf_op jit(solution)/shard_map/all_gather | solution.py:535
  111.8 4.5 all-to-all-start.1
  119.3 5.3 fusion.65
  124.9 5.3 fusion.196
  130.3 8.9 %multiply_convert_fusion.3 = (bf16[768,768]{1,0:T(8,128)(2,1)S(1)}, f32[768,768]{1,0:T(8,128)}, f32[768,768]{1,0:T(8,128)}) fusion(f32[768]{0:T(1024)S(1)} %copy-done.111, bf16[768,1344]{1,0:T(8,128)(2,1)} %bitcast.6, bf16[768,768]{1,0:T(8,128)(2,1)S(1)} %copy-done, f32[768]{0:T(1024)S(1)} %copy-done.107, f32[768]{0:T(1024)S(1)} %copy-done.104, ...), kind=kOutput, calls=%fused_computation.73 | convolution fusion | flops 948436992 | bytes 8272896 | tf_op jit(solution)/shard_map/dot_general | solution.py:493
  146.7 14.4 %all-gather.7.cloned.1.call-done = bf16[768,768]{1,0:T(8,128)(2,1)} async-done(((bf16[192,768]{1,0:T(8,128)(2,1)}), bf16[768,768]{1,0:T(8,128)(2,1)}) %all-gather.7.cloned.1.call-update) | async-done | bytes 1179664 | tf_op jit(solution)/shard_map/all_gather | solution.py:572
  163.6 70.1 %all-reduce.6.cloned.1.call-done = bf16[768,768]{1,0:T(8,128)(2,1)} async-done(((bf16[768,768]{1,0:T(8,128)(2,1)}), bf16[768,768]{1,0:T(8,128)(2,1)}) %all-reduce.6.cloned.1.call-update) | async-done | bytes 1179664 | tf_op jit(solution)/shard_map/psum | solution.py:591
  239.5 5.3 fusion.68
  246.4 7.4 fusion.198
  253.8 7.5 multiply_reduce_fusion.1
  270.9 5.9 fusion.72
  282.1 8.4 %multiply_convert_fusion.2 = (bf16[768,768]{1,0:T(8,128)(2,1)}, f32[768,768]{1,0:T(8,128)S(1)}, f32[768,768]{1,0:T(8,128)S(1)}) fusion(f32[768]{0:T(1024)S(1)} %copy-done.113, bf16[768,1344]{1,0:T(8,128)(2,1)} %bitcast.27, f32[768]{0:T(1024)S(1)} %copy-done.109, f32[768]{0:T(1024)S(1)} %copy-done.77, f32[768]{0:T(1024)S(1)} %copy-done.70, ...), kind=kOutput, calls=%fused_computation.56 | convolution fusion | flops 947847168 | bytes 9452544 | tf_op jit(solution)/shard_map/dot_general | solution.py:493
  315.5 39.7 %all-reduce.8.cloned.1.call-done = bf16[768,768]{1,0:T(8,128)(2,1)} async-done(((bf16[768,768]{1,0:T(8,128)(2,1)}), bf16[768,768]{1,0:T(8,128)(2,1)}) %all-reduce.8.cloned.1.call-update) | async-done | bytes 1179664 | tf_op jit(solution)/shard_map/psum | solution.py:634
  355.2 4.3 multiply_reduce_fusion.2
  382.3 5.7 fusion.76
  396.0 4.6 all-to-all-start.2
  418.4 5.1 fusion.176
  429.4 21.3 %all-to-all-done.2 = bf16[4,192,1344]{2,1,0:T(8,128)(2,1)} async-done(((bf16[4,192,1344]{2,1,0:T(8,128)(2,1)}), bf16[4,192,1344]{2,1,0:T(8,128)(2,1)}, u32[]{:S(2)}, u32[]{:S(2)}) %all-to-all-start.2) | async-done | bytes 2064416 | tf_op jit(solution)/shard_map/all_to_all | solution.py:650
  479.1 86.9 %all-reduce.12.cloned.1.call-done = (bf16[4,192,1344]{2,1,0:T(8,128)(2,1)}, bf16[4,192,1344]{2,1,0:T(8,128)(2,1)}, bf16[1,192,768]{2,1,0:T(8,128)(2,1)}, bf16[1,...) async-done(((bf16[4,192,1344]{2,1,0:T(8,128)(2,1)}, bf16[4,192,1344]{2,1,0:T(8,128)(2,1)}, bf16[1,192,768]{2,1,0:T(8,128)(2,1)}, ...) | async-done | bytes 7077904 | tf_op jit(solution)/shard_map/psum | solution.py:646
  566.1 4.9 all-to-all-start.3
  571.8 143.1 %all-reduce.10.cloned.1.call-done = f32[2,9216]{1,0:T(2,128)} async-done(((f32[2,9216]{1,0:T(2,128)}), f32[2,9216]{1,0:T(2,128)}) %all-reduce.10.cloned.1.call-update) | async-done | bytes 73744 | tf_op jit(solution)/shard_map/psum | solution.py:672
  719.2 29.7 %reduce-scatter.3.cloned.1.call-done = bf16[192,768]{1,0:T(8,128)(2,1)} async-done(((bf16[768,768]{1,0:T(8,128)(2,1)}), bf16[192,768]{1,0:T(8,128)(2,1)}) %reduce-scatter.3.cloned.1.call-update) | async-done | bytes 294928 | tf_op jit(solution)/shard_map/reduce_scatter | solution.py:594
  750.8 28.4 %reduce-scatter.5.cloned.1.call-done = bf16[192,768]{1,0:T(8,128)(2,1)} async-done(((bf16[768,768]{1,0:T(8,128)(2,1)}), bf16[192,768]{1,0:T(8,128)(2,1)}) %reduce-scatter.5.cloned.1.call-update) | async-done | bytes 294928 | tf_op jit(solution)/shard_map/reduce_scatter | solution.py:639
  (514 shorter events, 210.4 us)
Async XLA Ops:
  7.2 100.6 %all-gather.5.cloned.1.call-start = ((), (), s32[]{:S(2)}) async-start(), calls=%async_computation.6 | async-start | bytes 1474560 | tf_op jit(solution)/shard_map/all_gather | solution.py:533
  19.3 76.5 %copy-start.7 = (f32[192,768]{1,0:T(8,128)S(1)}, f32[192,768]{1,0:T(8,128)}, u32[]{:S(2)}) copy-start(f32[192,768]{1,0:T(8,128)} %param.25) | copy-start | bytes 1769476
  19.3 78.7 %copy-start.125 = (s32[1,8]{1,0:T(1,128)S(1)}, s32[1,8]{1,0:T(1,128)}, u32[]{:S(2)}) copy-start(s32[1,8]{1,0:T(1,128)} %param.14) | copy-start | bytes 100
  19.3 79.4 %copy-start.115 = (bf16[2,768]{1,0:T(2,128)(2,1)S(1)}, bf16[2,768]{1,0:T(2,128)(2,1)}, u32[]{:S(2)}) copy-start(bf16[2,768]{1,0:T(2,128)(2,1)} %param.22) | copy-start | bytes 9220
  19.3 79.4 %copy-start.5 = (bf16[1,192,2304]{2,1,0:T(8,128)(2,1)S(1)}, bf16[1,192,2304]{2,1,0:T(8,128)(2,1)}, u32[]{:S(2)}) copy-start(bf16[1,192,2304]{2,1,0:T(8,128)(2,1)} %get-tuple-element.71) | copy-start | bytes 2654212
  19.3 92.4 %all-to-all-start = ((bf16[4,192,1344]{2,1,0:T(8,128)(2,1)}), bf16[4,192,1344]{2,1,0:T(8,128)(2,1)}, u32[]{:S(2)}, u32[]{:S(2)}) async-start(bf16[4,192,1344]{2,1,0:T(8,128)(2,1)} %pad_maximum_fusion), calls=%async_computation | async-start | bytes 4325376 | tf_op jit(solution)/shard_map/all_to_all | solution.py:553
  25.8 135.2 %all-gather.7.cloned.1.call-start = ((), (), s32[]{:S(2)}) async-start(), calls=%async_computation.9 | async-start | bytes 1474560 | tf_op jit(solution)/shard_map/all_gather | solution.py:572
  111.2 19.1 %copy-start.72 = (f32[768]{0:T(1024)}, f32[768]{0:T(1024)S(1)}, u32[]{:S(2)}) copy-start(f32[768]{0:T(1024)S(1)} %add_rsqrt_fusion.1) | copy-start | bytes 9220
  111.8 124.7 %all-to-all-start.1 = ((bf16[4,192,1344]{2,1,0:T(8,128)(2,1)}), bf16[4,192,1344]{2,1,0:T(8,128)(2,1)}, u32[]{:S(2)}, u32[]{:S(2)}) async-start(bf16[4,192,1344]{2,1,0:T(8,128)(2,1)} %pad_maximum_fusion.1), calls=%async_computation.1 | async-start | bytes 4325376 | tf_op jit(solution)/shard_map/all_to_all | solution.py:553
  116.3 117.4 %all-reduce.6.cloned.1.call-start = ((), (), s32[]{:S(2)}) async-start(), calls=%async_computation.7 | async-start | bytes 2359296 | tf_op jit(solution)/shard_map/psum | solution.py:591
  144.2 211.0 %all-reduce.8.cloned.1.call-start = ((), (), s32[]{:S(2)}) async-start(), calls=%async_computation.10 | async-start | bytes 2359296 | tf_op jit(solution)/shard_map/psum | solution.py:634
  279.2 16.2 %copy-start.1 = (f32[768,768]{1,0:T(8,128)}, f32[768,768]{1,0:T(8,128)S(1)}, u32[]{:S(2)}) copy-start(f32[768,768]{1,0:T(8,128)S(1)} %fusion.113) | copy-start | bytes 7077892
  396.0 54.7 %all-to-all-start.2 = ((bf16[4,192,1344]{2,1,0:T(8,128)(2,1)}), bf16[4,192,1344]{2,1,0:T(8,128)(2,1)}, u32[]{:S(2)}, u32[]{:S(2)}) async-start(bf16[4,192,1344]{2,1,0:T(8,128)(2,1)} %bitcast.231), calls=%async_computation.4 | async-start | bytes 4325376 | tf_op jit(solution)/shard_map/all_to_all | solution.py:650
  400.6 165.5 %all-reduce.12.cloned.1.call-start = ((), (), s32[]{:S(2)}) async-start(), calls=%async_computation.13 | async-start | bytes 14548992 | tf_op jit(solution)/shard_map/psum | solution.py:646
  450.7 22.1 %copy-start.68 = (f32[3072]{0:T(1024)S(1)}, f32[3072]{0:T(1024)}, u32[]{:S(2)}) copy-start(f32[3072]{0:T(1024)} %dynamic_update_slice.39) | copy-start | bytes 36868
  450.7 24.3 %copy-start.23 = (bf16[2,192,768]{2,1,0:T(8,128)(2,1)S(1)}, bf16[2,192,768]{2,1,0:T(8,128)(2,1)}, u32[]{:S(2)}) copy-start(bf16[2,192,768]{2,1,0:T(8,128)(2,1)} %param.19) | copy-start | bytes 1769476
  450.7 264.2 %all-reduce.10.cloned.1.call-start = ((), (), s32[]{:S(2)}) async-start(), calls=%async_computation.12 | async-start | bytes 147456 | tf_op jit(solution)/shard_map/psum | solution.py:672
  474.9 274.0 %reduce-scatter.3.cloned.1.call-start = ((), (), s32[]{:S(2)}) async-start(), calls=%async_computation.8 | async-start | bytes 1474560 | tf_op jit(solution)/shard_map/reduce_scatter | solution.py:594
  478.4 300.8 %reduce-scatter.5.cloned.1.call-start = ((), (), s32[]{:S(2)}) async-start(), calls=%async_computation.11 | async-start | bytes 1474560 | tf_op jit(solution)/shard_map/reduce_scatter | solution.py:639
  479.1 91.8 %copy-start.83 = (f32[4,192]{1,0:T(4,128)S(1)}, f32[4,192]{1,0:T(4,128)}, u32[]{:S(2)}) copy-start(f32[4,192]{1,0:T(4,128)} %get-tuple-element.28) | copy-start | bytes 9220
  566.1 227.3 %all-to-all-start.3 = ((bf16[4,192,1344]{2,1,0:T(8,128)(2,1)}), bf16[4,192,1344]{2,1,0:T(8,128)(2,1)}, u32[]{:S(2)}, u32[]{:S(2)}) async-start(bf16[4,192,1344]{2,1,0:T(8,128)(2,1)} %get-tuple-element.42), calls=%async_computation.5 | async-start | bytes 4325376 | tf_op jit(solution)/shard_map/all_to_all | solution.py:647
  570.9 209.6 %copy-start.8 = (f32[192,768]{1,0:T(8,128)S(1)}, f32[192,768]{1,0:T(8,128)}, u32[]{:S(2)}) copy-start(f32[192,768]{1,0:T(8,128)} %param.25) | copy-start | bytes 1769476
  716.5 92.8 %copy-start.91 = (f32[2,192]{1,0:T(2,128)}, f32[2,192]{1,0:T(2,128)S(1)}, u32[]{:S(2)}) copy-start(f32[2,192]{1,0:T(2,128)S(1)} %constant_dynamic-slice_fusion.2) | copy-start | bytes 4612
  750.8 32.1 %copy-start.11 = (bf16[4,192,1344]{2,1,0:T(8,128)(2,1)S(1)}, bf16[4,192,1344]{2,1,0:T(8,128)(2,1)}, u32[]{:S(2)}) copy-start(bf16[4,192,1344]{2,1,0:T(8,128)(2,1)} %get-tuple-element.43) | copy-start | bytes 6193156
  (126 other events, 521.7 us)
Sparse Core Ops, SparseCore 0:
  9.6 51.4 all-gather.4
  111.9 49.1 all-gather.6
  164.0 69.6 all-reduce.5
  299.7 55.4 all-reduce.7
  450.9 115.1 all-reduce.11
  572.1 142.8 all-reduce.9
  717.8 31.0 reduce-scatter.2
  751.2 27.8 reduce-scatter.4
